TPU v7x, 32 devices: a whole 2x2x4 slice. The times are simulated.
32 devices in a mesh: scan: 2 (over x), slab: 16 (over z, y, core).
Axes of the slice: x: 2, y: 2, z: 4, core: 2. Of those that a mesh axis runs over, the one named last changes fastest.
Arguments:
- image_coef: float32 [4, 12, 128, 384], P('scan', None, 'slab'), parts along dimension 0, may hold values from -6 to 6
- step_coef: float32 [4, 12, 128, 384], P('scan', None, 'slab'), parts along dimension 0, may hold values from -6 to 6
- coil_spec: float32 [96, 128, 384], P(('scan', 'slab')), parts along dimension 0, may hold values from -24 to 24
- step_spec: float32 [96, 128, 384], P(('scan', 'slab')), parts along dimension 0, may hold values from -12 to 12
- temporal_basis: float32 [30, 12], replicated, may hold values from -1 to 1
- sample_mask: int32 [256, 192], P('scan'), parts along dimension 0, may hold values from 0 to 1073741823, as said below
Outputs:
- grad_coef: float32 [4, 12, 128, 384], P('scan', None, 'slab'), parts along dimension 0
- grad_spec: float32 [96, 128, 384], P(('scan', 'slab')), parts along dimension 0
There are 2 independent parts, one for each index of `scan`. A program takes and returns all parts, laid end to end along the dimension named above; an argument that names none is the same for every part. Nothing has to cross between parts.
Inputs may be any that keep to these rules, and one draw needn't show every extreme that they name: `sample_mask`: bit t of the entry for spectral point (kz, ky) is 1 where frame t samples that point, bits 30 and above are 0; the 7 x 7 points nearest the centre of k-space are sampled in every frame.
All inputs are finite; a program needn't handle non-finite values.
Results may differ from a plain program's by a relative error of at most 0.000071.
Values sent between devices are 32-bit elements; how exact they have to be, the bound alone decides.
A program may use at most 128 MiB of HBM per device.

v0:
```python
import functools
import math

import jax
import jax.numpy as jnp
import ml_dtypes
import numpy as np
from jax import lax
from jax.experimental import pallas as pl
from jax.experimental.pallas import tpu as pltpu
from jax.sharding import PartitionSpec as P

NY = 192
NZ = 128
HY = NY // 2
COEFS = 12
FRAMES = 30
ALPHA = 0.5
SOBOLEV = 32.0
PAIRS = [(a, b) for a in range(COEFS) for b in range(a, COEFS)]
PAIR_AT = {p: i for i, p in enumerate(PAIRS)}
F32 = jnp.float32
BF16 = jnp.bfloat16


def complex_table(rows, cols, length, sign):
    idx = (np.asarray(rows)[:, None] * np.asarray(cols)[None, :]) % length
    angles = 2.0 * math.pi * idx / length
    scale = 1.0 / math.sqrt(length)
    return np.cos(angles) * scale, np.sin(angles) * (scale * sign)


def split_np(table):
    high = table.astype(np.float32).astype(ml_dtypes.bfloat16)
    low = (table - high.astype(np.float64)).astype(np.float32).astype(ml_dtypes.bfloat16)
    return high, low


def right_table(length, sign):
    c, s = complex_table(range(length), range(length), length, sign)
    high, low = split_np(np.block([[c, s], [-s, c]]))
    return np.concatenate([high, low, high], axis=0)


def left_table(rows, cols, length, sign):
    c, s = complex_table(rows, cols, length, sign)
    high, low = split_np(np.block([[c, -s], [s, c]]))
    return np.concatenate([high, high, low], axis=1)


EVEN = np.arange(0, NY, 2)
ODD = np.arange(1, NY, 2)
NEAR = np.arange(HY)


def make_tables():
    y_left = np.stack(
        [
            left_table(EVEN, NEAR, NY, -1.0),
            left_table(ODD, NEAR, NY, -1.0),
            left_table(NEAR, EVEN, NY, 1.0),
            left_table(NEAR, ODD, NY, 1.0),
        ]
    )
    y_right = np.stack([right_table(NY, -1.0), right_table(NY, 1.0)])
    z_right = np.stack([right_table(NZ, -1.0), right_table(NZ, 1.0)])
    fz = ((np.arange(NZ) + NZ // 2) % NZ - NZ // 2) / NZ
    fy = ((np.arange(NY) + NY // 2) % NY - NY // 2) / NY
    plane = 1.0 / (1.0 + SOBOLEV * (fz[:, None] ** 2 + fy[None, :] ** 2)) ** 2
    weights = np.concatenate([plane, plane], axis=1).astype(np.float32)
    return y_left, y_right, z_right, weights


def split(x):
    high = x.astype(BF16)
    low = (x - high.astype(F32)).astype(BF16)
    return high, low


def times_right(x, table):
    high, low = split(x)
    return jnp.dot(jnp.concatenate([high, high, low], axis=1), table, preferred_element_type=F32)


def times_left(table, x):
    high, low = split(x)
    return jnp.dot(table, jnp.concatenate([high, low, high], axis=0), preferred_element_type=F32)


def z_stage(re, im, table):
    out = times_right(jnp.concatenate([re, im], axis=1), table)
    return out[:, :NZ], out[:, NZ:]


def forward(planes, yl, zt):
    ups, downs = [], []
    for re, im in planes:
        ups.append(jnp.concatenate([re[:HY] + re[HY:], im[:HY] + im[HY:]], axis=0))
        downs.append(jnp.concatenate([re[:HY] - re[HY:], im[:HY] - im[HY:]], axis=0))
    even = times_left(yl[0], jnp.concatenate(ups, axis=1))
    odd = times_left(yl[1], jnp.concatenate(downs, axis=1))
    outs = []
    for i in range(2):
        at = slice(i * NZ, (i + 1) * NZ)
        re = jnp.concatenate([even[:HY, at], odd[:HY, at]], axis=0)
        im = jnp.concatenate([even[HY:, at], odd[HY:, at]], axis=0)
        outs.append(z_stage(re, im, zt[0]))
    return outs


def inverse(planes, yl, zt):
    evens, odds = [], []
    for re, im in planes:
        re, im = z_stage(re, im, zt[1])
        evens.append(jnp.concatenate([re[:HY], im[:HY]], axis=0))
        odds.append(jnp.concatenate([re[HY:], im[HY:]], axis=0))
    even = times_left(yl[2], jnp.concatenate(evens, axis=1))
    odd = times_left(yl[3], jnp.concatenate(odds, axis=1))
    near, far = even + odd, even - odd
    outs = []
    for i in range(2):
        at = slice(i * NZ, (i + 1) * NZ)
        re = jnp.concatenate([near[:HY, at], far[:HY, at]], axis=0)
        im = jnp.concatenate([near[HY:, at], far[HY:, at]], axis=0)
        outs.append((re, im))
    return outs


def coil_images(items, coil_ref, step_ref, weights, yr, zt, img):
    @pl.loop(0, items)
    def _(i):
        for which, ref in enumerate((coil_ref, step_ref)):
            rows = times_right(ref[i] * weights[...], yr[1])
            t = rows.T
            re, im = z_stage(t[:NY], t[NY:], zt[1])
            img[i, which, 0] = re
            img[i, which, 1] = im


def transposed_in(cols, colt, first, count):
    @pl.loop(first, first + count)
    def _(p):
        colt[p] = cols[p].T.reshape(2, NY, NZ)


def forward_pass(items, first_pair, pair_count, colt, img, spec, yl, zt):
    @pl.loop(first_pair * items, (first_pair + pair_count) * items)
    def _(step):
        pair, i = step // items, step % items
        planes = []
        for j in range(2):
            k = 2 * pair + j
            cr, ci = colt[2 * k, 0], colt[2 * k, 1]
            sr, si = colt[2 * k + 1, 0], colt[2 * k + 1, 1]
            ar, ai = img[i, 0, 0], img[i, 0, 1]
            dr, di = img[i, 1, 0], img[i, 1, 1]
            planes.append((ar * sr - ai * si + dr * cr - di * ci, ar * si + ai * sr + dr * ci + di * cr))
        for j, (re, im) in enumerate(forward(planes, yl, zt)):
            spec[i, 2 * pair + j, 0] = re
            spec[i, 2 * pair + j, 1] = im


def mix_pass(items, gram, spec):
    @pl.loop(0, NY // 8)
    def _(tile):
        rows = pl.ds(pl.multiple_of(tile * 8, 8), 8)
        for i in range(items):
            re = [spec[i, k, 0, rows, :] for k in range(COEFS)]
            im = [spec[i, k, 1, rows, :] for k in range(COEFS)]
            for k in range(COEFS):
                acc_re = acc_im = None
                for m in range(COEFS):
                    g = gram[PAIR_AT[(min(k, m), max(k, m))], rows, :]
                    acc_re = g * re[m] if acc_re is None else acc_re + g * re[m]
                    acc_im = g * im[m] if acc_im is None else acc_im + g * im[m]
                spec[i, k, 0, rows, :] = acc_re
                spec[i, k, 1, rows, :] = acc_im


def inverse_pass(items, first_pair, pair_count, colt, img, spec, grad, back, yl, zt):
    @pl.loop(first_pair * items, (first_pair + pair_count) * items)
    def _(step):
        pair, i = step // items, step % items
        outs = inverse([(spec[i, 2 * pair + j, 0], spec[i, 2 * pair + j, 1]) for j in range(2)], yl, zt)
        ar, ai = img[i, 0, 0], img[i, 0, 1]
        back_re, back_im = back[i, 0], back[i, 1]
        for j, (re, im) in enumerate(outs):
            k = 2 * pair + j
            cr, ci = colt[2 * k, 0], colt[2 * k, 1]
            back_re += cr * re + ci * im
            back_im += cr * im - ci * re
            grad_re = ar * re + ai * im
            grad_im = ar * im - ai * re

            @pl.when(i == 0)
            def _():
                grad[k, 0] = grad_re
                grad[k, 1] = grad_im

            @pl.when(i > 0)
            def _():
                grad[k, 0] += grad_re
                grad[k, 1] += grad_im

        back[i, 0] = back_re
        back[i, 1] = back_im


def coil_gradients(items, back, step_ref, weights, yr, zt, out):
    @pl.loop(0, items)
    def _(i):
        re, im = z_stage(back[i, 0], back[i, 1], zt[0])
        rows = jnp.concatenate([re, im], axis=0).T
        out[i] = times_right(rows, yr[0]) * weights[...] + ALPHA * step_ref[i]


def compute_kernel(items, cols, coil, step, gram, yl, yr, zt, weights, part, spec_out, colt, img, spec, grad, back):
    coil_images(items, coil, step, weights, yr, zt, img)
    transposed_in(cols, colt, 0, 2 * COEFS)
    back[...] = jnp.zeros_like(back)
    forward_pass(items, 0, COEFS // 2, colt, img, spec, yl, zt)
    mix_pass(items, gram, spec)
    inverse_pass(items, 0, COEFS // 2, colt, img, spec, grad, back, yl, zt)

    @pl.loop(0, COEFS)
    def _(k):
        part[k] = grad[k].reshape(2 * NY, NZ).T

    coil_gradients(items, back, step, weights, yr, zt, spec_out)


def compute(cols, coil, step, gram):
    items = coil.shape[0]
    tables = make_tables()
    vmem = pl.BlockSpec(memory_space=pltpu.VMEM)
    return pl.pallas_call(
        functools.partial(compute_kernel, items),
        out_shape=(
            jax.ShapeDtypeStruct((COEFS, NZ, 2 * NY), F32),
            jax.ShapeDtypeStruct(coil.shape, F32),
        ),
        in_specs=[vmem] * 8,
        out_specs=(vmem, vmem),
        scratch_shapes=[
            pltpu.VMEM((2 * COEFS, 2, NY, NZ), F32),
            pltpu.VMEM((items, 2, 2, NY, NZ), F32),
            pltpu.VMEM((items, COEFS, 2, NY, NZ), F32),
            pltpu.VMEM((COEFS, 2, NY, NZ), F32),
            pltpu.VMEM((items, 2, NY, NZ), F32),
        ],
        compiler_params=pltpu.CompilerParams(vmem_limit_bytes=56 * 2**20),
        cost_estimate=pl.CostEstimate(flops=16 * 10**9, bytes_accessed=20 * 2**20, transcendentals=0),
    )(cols, coil, step, gram, *[jnp.asarray(t) for t in tables])


def gram_planes(temporal_basis, sample_mask):
    first = np.array([p[0] for p in PAIRS])
    second = np.array([p[1] for p in PAIRS])
    outer = (temporal_basis[:, first] * temporal_basis[:, second]).T
    mask = sample_mask.T.reshape(HY, 2, NZ).transpose(1, 0, 2).reshape(NY, NZ)
    frames = jnp.arange(FRAMES, dtype=jnp.int32)
    bits = jnp.bitwise_and(jnp.right_shift(mask[None], frames[:, None, None]), 1).astype(F32)
    return jnp.einsum("qt,tyz->qyz", outer, bits, precision=lax.Precision.HIGHEST)


def gather_plain(both, devices):
    width_x = both.shape[0]
    groups = devices // width_x
    rep = jnp.broadcast_to(both[:, None], (width_x, groups) + both.shape[1:])
    rep = rep.reshape((devices * both.shape[1],) + both.shape[2:])
    return lax.all_to_all(rep, "slab", split_axis=0, concat_axis=1, tiled=True)


def scatter_plain(part, width_x, devices):
    homed = lax.all_to_all(part, "slab", split_axis=1, concat_axis=0, tiled=True)
    rows = part.shape[1] // devices
    return jnp.sum(homed.reshape(width_x, devices // width_x, COEFS, rows, 2 * NY), axis=1)


def shards(image_coef, step_coef, coil_spec, step_spec, temporal_basis, sample_mask):
    devices = lax.axis_size("slab")
    width_x, _, rows_z, _ = image_coef.shape
    both = jnp.stack([image_coef, step_coef], axis=2).reshape(width_x, 2 * COEFS, rows_z, 2 * NY)
    cols = gather_plain(both, devices)
    gram = gram_planes(temporal_basis, sample_mask)
    part, grad_spec = compute(cols, coil_spec, step_spec, gram)
    grad_coef = scatter_plain(part, width_x, devices) + ALPHA * step_coef
    return grad_coef, grad_spec


def solution(mesh):
    in_specs = (
        P("scan", None, "slab", None),
        P("scan", None, "slab", None),
        P(("scan", "slab"), None, None),
        P(("scan", "slab"), None, None),
        P(),
        P("scan", None),
    )
    out_specs = (P("scan", None, "slab", None), P(("scan", "slab"), None, None))
    return jax.shard_map(shards, mesh=mesh, in_specs=in_specs, out_specs=out_specs, check_vma=False)
```

profile of v0, /device:TPU:0, one launch (start us, length us, event | category | flops | bytes accessed | tf_op | source)
XLA Modules:
  0.0 251.7 jit_solution(1831157301199290459)
XLA Ops:
  0.6 0.0 copy-start
  0.6 1.1 pad_maximum_fusion
  1.7 2.6 %broadcast_in_dim.15 = f32[2,8,24,8,384]{4,3,2,1,0:T(8,128)} broadcast(f32[2,24,8,384]{3,2,1,0:T(8,128)S(1)} %bitcast.29), dimensions={0,2,3,4} | broadcast | bytes 5308416 | tf_op jit(solution)/shard_map/broadcast_in_dim | solution.py:269
  4.3 0.0 copy-start.1
  4.3 0.0 copy-start.2
  4.3 0.0 copy-start.3
  4.3 7.6 %all-to-all-start = ((f32[384,8,384]{2,1,0:T(8,128)}), f32[384,8,384]{2,1,0:T(8,128)}, u32[]{:S(2)}, u32[]{:S(2)}) async-start(f32[384,8,384]{2,1,0:T(8,128)} %bitcast.26), calls=%async_computation | async-start | bytes 9437184 | tf_op jit(solution)/shard_map/all_to_all | solution.py:271
  11.9 0.0 copy-done.1
  11.9 0.0 copy-done.2
  11.9 0.0 copy-done
  11.9 0.6 gather_fusion
  12.5 0.0 copy-done.3
  12.6 0.6 gather_fusion.1
  13.2 6.6 %fusion = f32[78,192,128]{2,0,1:T(8,128)S(1)} fusion(s32[192,128]{1,0:T(8,128)S(1)} %bitcast.31, f32[78,30]{1,0:T(8,128)S(1)} %gather_fusion, f32[78,30]{1,0:T(8,128)S(1)} %gather_fusion.1), kind=kOutput, calls=%fused_computation.3 | convolution fusion | flops 692308224 | bytes 7784736 | tf_op jit(solution)/shard_map/qt,tyz->qyz/dot_general | solution.py:263
  19.7 5.4 %copy.28.gram = f32[78,192,128]{2,1,0:T(8,128)} copy(f32[78,192,128]{2,0,1:T(8,128)S(1)} %fusion) | data formatting | bytes 15335424 | tf_op jit(solution)/shard_map/qt,tyz->qyz/dot_general | solution.py:263
  25.1 73.6 %all-to-all-done = f32[384,8,384]{2,1,0:T(8,128)} async-done(((f32[384,8,384]{2,1,0:T(8,128)}), f32[384,8,384]{2,1,0:T(8,128)}, u32[]{:S(2)}, u32[]{:S(2)}) %all-to-all-start) | async-done | bytes 4718624 | tf_op jit(solution)/shard_map/all_to_all | solution.py:271
  98.7 5.0 %copy.41 = f32[24,16,8,384]{3,2,1,0:T(8,128)} copy(f32[24,16,8,384]{3,2,0,1:T(8,128)} %bitcast.5) | data formatting | bytes 9437184 | tf_op jit(solution)/shard_map/all_to_all | solution.py:271
  103.7 51.6 %shard_map.149 = (f32[12,128,384]{2,1,0:T(8,128)}, f32[3,128,384]{2,1,0:T(8,128)}) custom-call(f32[24,128,384]{2,1,0:T(8,128)} %bitcast.28, f32[3,128,384]{2,1,0:T(8,128)} %coil.1, f32[3,128,384]{2,1,0:T(8,128)} %step.1, f32[78,192,128]{2,1,0:T(8,128)} %copy.28.gram, bf16[4,192,576]{2,1,0:T(8,128)(2,1)} %constant.25.clone.yl, ...), custom_call_target="tpu_custom_call" | custom-call | flops 16000000000 | bytes 20971520 | tf_op jit(solution)/shard_map/pallas_call | solution.py:236
  155.2 3.1 %copy.29 = f32[12,128,384]{2,0,1:T(8,128)S(1)} copy(f32[12,128,384]{2,1,0:T(8,128)} %get-tuple-element.4) | data formatting | bytes 4718592 | tf_op jit(solution)/shard_map/pallas_call | solution.py:236
  158.3 91.3 %all_to_all.33 = f32[12,128,384]{2,0,1:T(8,128)S(1)} all-to-all(f32[12,128,384]{2,0,1:T(8,128)S(1)} %copy.29), channel_id=1, replica_groups=mesh['scan'=2,'slab'=16] {'slab'}, dimensions={1} | all-to-all | bytes 4718592 | tf_op jit(solution)/shard_map/all_to_all | solution.py:275
  249.7 0.2 reduce
  249.9 1.1 copy_add_fusion
  251.0 0.7 copy.32
  (3 shorter events, 0.0 us)
Async XLA Ops:
  0.6 11.3 %copy-start = (f32[30,12]{0,1:T(8,128)S(1)}, f32[30,12]{0,1:T(8,128)}, u32[]{:S(2)}) copy-start(f32[30,12]{0,1:T(8,128)} %param.18) | copy-start | bytes 4324
  4.3 7.6 %copy-start.1 = (s32[128,192]{0,1:T(8,128)S(1)}, s32[128,192]{0,1:T(8,128)}, u32[]{:S(2)}) copy-start(s32[128,192]{0,1:T(8,128)} %param.19) | copy-start | bytes 294916
  4.3 7.6 %copy-start.2 = (s32[78]{0:T(128)S(1)}, s32[78]{0:T(128)}, u32[]{:S(2)}) copy-start(s32[78]{0:T(128)} %constant.35) | copy-start | bytes 940
  4.3 8.2 %copy-start.3 = (s32[78]{0:T(128)S(1)}, s32[78]{0:T(128)}, u32[]{:S(2)}) copy-start(s32[78]{0:T(128)} %constant.36) | copy-start | bytes 940
  4.3 94.4 %all-to-all-start = ((f32[384,8,384]{2,1,0:T(8,128)}), f32[384,8,384]{2,1,0:T(8,128)}, u32[]{:S(2)}, u32[]{:S(2)}) async-start(f32[384,8,384]{2,1,0:T(8,128)} %bitcast.26), calls=%async_computation | async-start | bytes 9437184 | tf_op jit(solution)/shard_map/all_to_all | solution.py:271
where the time goes:
time: 252 us
  blocking collectives  91.3 us (36%)
  waiting for transfers between devices  73.6 us (29%)
  Pallas kernels  51.6 us (20%)
  local copies, waits for them, and re-layouts  18 us (7%)
  starting transfers between devices  7.56 us (3%)
  matrix products  6.56 us (3%)
    all_to_all x1, blocking collectives, scatter_plain(): lax.all_to_all(part, 'slab', split_axis=1, concat_axis=0, tiled=True)  91.3 us
    all_to_all x1, waiting for transfers between devices, gather_plain(): return lax.all_to_all(rep, 'slab', split_axis=0, concat_axis=1, tiled=True)  73.6 us
    pallas_call x1, Pallas kernels, compute(): pl.pallas_call(functools.partial(compute_kernel, items), out_shape=(jax.S...  51.6 us
    all_to_all x1, starting transfers between devices, gather_plain(): return lax.all_to_all(rep, 'slab', split_axis=0, concat_axis=1, tiled=True)  7.56 us
    dot_general x1, matrix products, gram_planes(): jnp.einsum('qt,tyz->qyz', outer, bits, precision=lax.Precision.HIGHEST)  6.56 us
    dot_general x1, local copies, waits for them, and re-layouts, gram_planes(): jnp.einsum('qt,tyz->qyz', outer, bits, precision=lax.Precision.HIGHEST)  5.38 us
  transfers between devices with their start and end apart: 1, of which 1 were waited for; matrix products, arithmetic and copies ran while one was open for 5% of the time, Pallas kernels for 0%

commit v1 on v0

--- a/solution.py
+++ b/solution.py
@@ -277,14 +277,354 @@
     return jnp.sum(homed.reshape(width_x, devices // width_x, COEFS, rows, 2 * NY), axis=1)
 
 
+MESH = pl.DeviceIdType.MESH
+
+
+class Place:
+    def __init__(self):
+        me = lax.axis_index("slab")
+        self.z, self.y, self.c = me // 4, (me // 2) % 2, me % 2
+        self.half = self.z // 2
+        self.pair = 4 * self.half + 1 - self.z
+        self.near = 2 - self.half
+        self.far = 3 - 3 * self.half
+        self.gate = self.z == 1 + self.half
+
+    def slab(self, z=None, y=None, c=None):
+        z = self.z if z is None else z
+        y = self.y if y is None else y
+        c = self.c if c is None else c
+        return z * 4 + y * 2 + c
+
+
+def rcopy(src, dst, send, recv, slab):
+    return pltpu.make_async_remote_copy(
+        src_ref=src, dst_ref=dst, send_sem=send, recv_sem=recv, device_id={"slab": slab}, device_id_type=MESH
+    )
+
+
+def greet(at):
+    barrier = pltpu.get_barrier_semaphore()
+
+    def hello(slab):
+        pl.semaphore_signal(barrier, inc=1, device_id={"slab": slab}, device_id_type=MESH)
+
+    hello(at.slab(z=at.pair))
+    hello(at.slab(y=1 - at.y))
+    hello(at.slab(c=1 - at.c))
+    hello(at.slab(z=at.near))
+
+    @pl.when(at.gate)
+    def _():
+        hello(at.slab(z=at.far))
+        pl.semaphore_wait(barrier, 5)
+
+    @pl.when(jnp.logical_not(at.gate))
+    def _():
+        pl.semaphore_wait(barrier, 4)
+
+
+class Gather:
+    def __init__(self, at, both, cols, sems, chunks):
+        self.at, self.both, self.cols, self.chunks = at, both, cols, chunks
+        self.own_sem, self.zs, self.zr, self.fs, self.ys, self.yr, self.cs, self.cr = sems
+        self.size = 2 * COEFS // chunks
+
+    def block(self, ch, z, y=None, c=None):
+        at = self.at
+        return self.cols.at[
+            pl.ds(ch * self.size, self.size), z, at.y if y is None else y, at.c if c is None else c
+        ]
+
+    def mine(self, ch, x):
+        return self.both.at[x, pl.ds(ch * self.size, self.size)]
+
+    def own(self, ch):
+        return pltpu.make_async_copy(self.mine(ch, self.at.half), self.block(ch, self.at.z), self.own_sem.at[ch])
+
+    def to_pair(self, ch):
+        at = self.at
+        return rcopy(
+            self.mine(ch, at.half), self.block(ch, at.z), self.zs.at[ch, 0], self.zr.at[ch, at.z], at.slab(z=at.pair)
+        )
+
+    def to_gate(self, ch):
+        at = self.at
+        return rcopy(
+            self.mine(ch, 1 - at.half), self.block(ch, at.z), self.zs.at[ch, 1], self.zr.at[ch, at.z], at.slab(z=at.near)
+        )
+
+    def onward(self, ch, z, i):
+        at = self.at
+        return rcopy(self.block(ch, z), self.block(ch, z), self.fs.at[ch, i], self.zr.at[ch, z], at.slab(z=at.pair))
+
+    def z_arrival(self, ch, z):
+        return rcopy(self.block(ch, z), self.block(ch, z), self.fs.at[ch, 0], self.zr.at[ch, z], self.at.slab(z=self.at.pair))
+
+    def across(self, ch, z, src=None):
+        at = self.at
+        src = self.block(ch, z) if src is None else src
+        return rcopy(src, self.block(ch, z), self.ys.at[ch, z], self.yr.at[ch, z], at.slab(y=1 - at.y))
+
+    def y_arrival(self, ch, z):
+        at = self.at
+        dst = self.block(ch, z, y=1 - at.y)
+        return rcopy(dst, dst, self.ys.at[ch, z], self.yr.at[ch, z], at.slab(y=1 - at.y))
+
+    def core(self, ch, c=None):
+        at = self.at
+        dst = self.cols.at[pl.ds(ch * self.size, self.size), :, :, at.c if c is None else c]
+        return rcopy(dst, dst, self.cs.at[ch], self.cr.at[ch], at.slab(c=1 - at.c))
+
+    def start(self, ch):
+        self.own(ch).start()
+        self.to_gate(ch).start()
+        self.to_pair(ch).start()
+        self.across(ch, self.at.z, self.mine(ch, self.at.half)).start()
+
+    def on_z(self, ch):
+        at = self.at
+        self.z_arrival(ch, at.pair).wait_recv()
+        self.across(ch, at.pair).start()
+        for i, z in enumerate((at.near, at.far)):
+            self.z_arrival(ch, z).wait_recv()
+
+            @pl.when(at.gate)
+            def _():
+                self.onward(ch, z, i).start()
+
+            self.across(ch, z).start()
+
+    def on_y(self, ch):
+        self.own(ch).wait()
+        for z in range(4):
+            self.y_arrival(ch, z).wait_recv()
+        self.core(ch).start()
+
+    def on_core(self, ch):
+        self.core(ch, 1 - self.at.c).wait_recv()
+
+    def finish(self, ch):
+        at = self.at
+        self.to_gate(ch).wait_send()
+        self.to_pair(ch).wait_send()
+        self.across(ch, at.z, self.mine(ch, at.half)).wait_send()
+        for z in (at.pair, at.near, at.far):
+            self.across(ch, z).wait_send()
+
+        @pl.when(at.gate)
+        def _():
+            for i, z in enumerate((at.near, at.far)):
+                self.onward(ch, z, i).wait_send()
+
+        self.core(ch).wait_send()
+
+
+def gather_sems(chunks):
+    dma = pltpu.SemaphoreType.DMA
+    return [
+        dma((chunks,)),
+        dma((chunks, 2)),
+        dma((chunks, 4)),
+        dma((chunks, 2)),
+        dma((chunks, 4)),
+        dma((chunks, 4)),
+        dma((chunks,)),
+        dma((chunks,)),
+    ]
+
+
+class Scatter:
+    def __init__(self, at, part, step, out, bufs, sems, chunks):
+        self.at, self.part, self.step, self.out = at, part, step, out
+        self.from_core, self.from_y, self.from_z, self.from_far = bufs
+        self.cs, self.cr, self.ys, self.yr, self.zs, self.zr, self.fs, self.fr = sems
+        self.size = COEFS // chunks
+
+    def ks(self, ch):
+        return pl.ds(ch * self.size, self.size)
+
+    def core(self, ch):
+        at = self.at
+        return rcopy(
+            self.part.at[self.ks(ch), :, :, 1 - at.c],
+            self.from_core.at[self.ks(ch)],
+            self.cs.at[ch],
+            self.cr.at[ch],
+            at.slab(c=1 - at.c),
+        )
+
+    def across(self, ch):
+        at = self.at
+        return rcopy(
+            self.from_core.at[self.ks(ch), :, 1 - at.y],
+            self.from_y.at[self.ks(ch)],
+            self.ys.at[ch],
+            self.yr.at[ch],
+            at.slab(y=1 - at.y),
+        )
+
+    def inward(self, ch):
+        at = self.at
+        rows = pl.ds(1 - at.half, 3)
+        return rcopy(
+            self.from_y.at[self.ks(ch), rows],
+            self.from_z.at[self.ks(ch), rows],
+            self.zs.at[ch],
+            self.zr.at[ch],
+            at.slab(z=at.pair),
+        )
+
+    def outward(self, ch, z):
+        at = self.at
+        return rcopy(
+            self.from_y.at[self.ks(ch), z],
+            self.from_z.at[self.ks(ch), z],
+            self.zs.at[ch],
+            self.zr.at[ch],
+            at.slab(z=at.pair),
+        )
+
+    def home(self, ch, z, i):
+        at = self.at
+        return rcopy(
+            self.from_z.at[self.ks(ch), z], self.from_far.at[self.ks(ch)], self.fs.at[ch, i], self.fr.at[ch], at.slab(z=z)
+        )
+
+    def start(self, ch):
+        self.core(ch).start()
+
+    def on_core(self, ch):
+        at, ks = self.at, self.ks(ch)
+        self.core(ch).wait_recv()
+        self.from_core[ks] += self.part[ks, :, :, at.c]
+        self.across(ch).start()
+
+    def on_y(self, ch):
+        at, ks = self.at, self.ks(ch)
+        self.across(ch).wait_recv()
+        self.from_y[ks] += self.from_core[ks, :, at.y]
+
+        @pl.when(at.gate)
+        def _():
+            self.outward(ch, at.pair).start()
+
+        @pl.when(jnp.logical_not(at.gate))
+        def _():
+            self.inward(ch).start()
+
+    def on_z(self, ch):
+        at, ks = self.at, self.ks(ch)
+
+        @pl.when(at.gate)
+        def _():
+            self.inward(ch).wait_recv()
+            for i, z in enumerate((at.near, at.far)):
+                self.from_z[ks, z] += self.from_y[ks, z]
+                self.home(ch, z, i).start()
+
+        @pl.when(jnp.logical_not(at.gate))
+        def _():
+            self.outward(ch, at.z).wait_recv()
+
+        self.out[at.half, ks] = self.from_y[ks, at.z] + self.from_z[ks, at.z] + ALPHA * self.step[at.half, ks]
+
+    def on_far(self, ch):
+        at, ks = self.at, self.ks(ch)
+        self.home(ch, at.near, 0).wait_recv()
+        self.out[1 - at.half, ks] = self.from_far[ks] + ALPHA * self.step[1 - at.half, ks]
+
+    def finish(self, ch):
+        at = self.at
+        self.core(ch).wait_send()
+        self.across(ch).wait_send()
+
+        @pl.when(at.gate)
+        def _():
+            self.outward(ch, at.pair).wait_send()
+            for i, z in enumerate((at.near, at.far)):
+                self.home(ch, z, i).wait_send()
+
+        @pl.when(jnp.logical_not(at.gate))
+        def _():
+            self.inward(ch).wait_send()
+
+
+def scatter_scratch():
+    return [
+        pltpu.VMEM((COEFS, 4, 2, 8, 2 * NY), F32),
+        pltpu.VMEM((COEFS, 4, 8, 2 * NY), F32),
+        pltpu.VMEM((COEFS, 4, 8, 2 * NY), F32),
+        pltpu.VMEM((COEFS, 8, 2 * NY), F32),
+    ]
+
+
+def scatter_sems(chunks):
+    dma = pltpu.SemaphoreType.DMA
+    return [dma((chunks,))] * 6 + [dma((chunks, 2)), dma((chunks,))]
+
+
+def each(chunks, step):
+    @pl.loop(0, chunks)
+    def _(ch):
+        step(ch)
+
+
+def gather_kernel(chunks, both, cols, *sems):
+    at = Place()
+    greet(at)
+    g = Gather(at, both, cols, sems, chunks)
+    for step in (g.start, g.on_z, g.on_y, g.on_core, g.finish):
+        each(chunks, step)
+
+
+def gather_near(both):
+    chunks = 3
+    vmem = pl.BlockSpec(memory_space=pltpu.VMEM)
+    return pl.pallas_call(
+        functools.partial(gather_kernel, chunks),
+        out_shape=jax.ShapeDtypeStruct((2 * COEFS, 4, 2, 2, 8, 2 * NY), F32),
+        in_specs=[vmem],
+        out_specs=vmem,
+        scratch_shapes=gather_sems(chunks),
+        compiler_params=pltpu.CompilerParams(collective_id=0, has_side_effects=True, vmem_limit_bytes=32 * 2**20),
+    )(both)
+
+
+def scatter_kernel(chunks, part, step, out, *scratch):
+    at = Place()
+    greet(at)
+    s = Scatter(at, part, step, out, scratch[:4], scratch[4:], chunks)
+    for stage in (s.start, s.on_core, s.on_y, s.on_z, s.on_far, s.finish):
+        each(chunks, stage)
+
+
+def scatter_near(part, step):
+    chunks = 3
+    vmem = pl.BlockSpec(memory_space=pltpu.VMEM)
+    return pl.pallas_call(
+        functools.partial(scatter_kernel, chunks),
+        out_shape=jax.ShapeDtypeStruct(step.shape, F32),
+        in_specs=[vmem] * 2,
+        out_specs=vmem,
+        scratch_shapes=scatter_scratch() + scatter_sems(chunks),
+        compiler_params=pltpu.CompilerParams(collective_id=1, has_side_effects=True, vmem_limit_bytes=32 * 2**20),
+    )(part, step)
+
+
 def shards(image_coef, step_coef, coil_spec, step_spec, temporal_basis, sample_mask):
     devices = lax.axis_size("slab")
     width_x, _, rows_z, _ = image_coef.shape
     both = jnp.stack([image_coef, step_coef], axis=2).reshape(width_x, 2 * COEFS, rows_z, 2 * NY)
-    cols = gather_plain(both, devices)
     gram = gram_planes(temporal_basis, sample_mask)
-    part, grad_spec = compute(cols, coil_spec, step_spec, gram)
-    grad_coef = scatter_plain(part, width_x, devices) + ALPHA * step_coef
+    if devices == 16 and width_x == 2 and rows_z == 8:
+        cols = gather_near(both).reshape(2 * COEFS, NZ, 2 * NY)
+        part, grad_spec = compute(cols, coil_spec, step_spec, gram)
+        grad_coef = scatter_near(part.reshape(COEFS, 4, 2, 2, rows_z, 2 * NY), step_coef)
+    else:
+        cols = gather_plain(both, devices)
+        part, grad_spec = compute(cols, coil_spec, step_spec, gram)
+        grad_coef = scatter_plain(part, width_x, devices) + ALPHA * step_coef
     return grad_coef, grad_spec
 
 

time: 252 us -> 135 us (0.54)
  blocking collectives: 91.3 us -> 0 us
  waiting for transfers between devices: 73.6 us -> 0 us
  Pallas kernels: 51.6 us -> 114 us
  starting transfers between devices: 7.56 us -> 0 us
  local copies, waits for them, and re-layouts: 18 us -> 12.1 us
    all_to_all x1 -> x0, blocking collectives: 91.3 us -> none  [scatter_plain(): lax.all_to_all(part, 'slab', split_axis=1, concat_axis=0, tiled=True)]
    all_to_all x1 -> x0, waiting for transfers between devices: 73.6 us -> none  [gather_plain(): return lax.all_to_all(rep, 'slab', split_axis=0, concat_axis=1, tiled=True)]
    pallas_call x0 -> x2, Pallas kernels: none -> 63.5 us  [the longest x1 36.1 us: gather_near(): pl.pallas_call(functools.partial(gather_kernel, chunks), out_shape=jax.Sh...]
    all_to_all x1 -> x0, starting transfers between devices: 7.56 us -> none  [gather_plain(): return lax.all_to_all(rep, 'slab', split_axis=0, concat_axis=1, tiled=True)]
    all_to_all x1 -> x0, local copies, waits for them, and re-layouts: 4.99 us -> none  [gather_plain(): return lax.all_to_all(rep, 'slab', split_axis=0, concat_axis=1, tiled=True)]
    unnamed x9 -> x11, local copies, waits for them, and re-layouts: 0.75 us -> 4.54 us
    pallas_call x1 -> x0, local copies, waits for them, and re-layouts: 3.08 us -> none  [compute(): pl.pallas_call(functools.partial(compute_kernel, items), out_shape=(jax.S...]
    broadcast_in_dim x1 -> x0, local copies, waits for them, and re-layouts: 2.56 us -> none  [gather_plain(): rep = jnp.broadcast_to(both[:, None], (width_x, groups) + both.shape[1:])]
  transfers between devices with their start and end apart: 1 -> 0, of which waited for: 1 -> 0; matrix products, arithmetic and copies ran while one was open for 5% -> 0% of each run, Pallas kernels for 0% -> 0%
where the time goes in v1:
time: 135 us
  Pallas kernels  114 us (84%)
  local copies, waits for them, and re-layouts  12.1 us (9%)
  matrix products  6.32 us (5%)
  other arithmetic  1.36 us (1%)
    pallas_call x1, Pallas kernels, compute(): pl.pallas_call(functools.partial(compute_kernel, items), out_shape=(jax.S...  50.6 us
    pallas_call x1, Pallas kernels, gather_near(): pl.pallas_call(functools.partial(gather_kernel, chunks), out_shape=jax.Sh...  36.1 us
    pallas_call x1, Pallas kernels, scatter_near(): pl.pallas_call(functools.partial(scatter_kernel, chunks), out_shape=jax.S...  27.4 us
    dot_general x1, matrix products, gram_planes(): jnp.einsum('qt,tyz->qyz', outer, bits, precision=lax.Precision.HIGHEST)  6.32 us
    dot_general x1, local copies, waits for them, and re-layouts, gram_planes(): jnp.einsum('qt,tyz->qyz', outer, bits, precision=lax.Precision.HIGHEST)  5.37 us
    unnamed x11, local copies, waits for them, and re-layouts  4.54 us

profile of v1, /device:TPU:0, one launch (start us, length us, event | category | flops | bytes accessed | tf_op | source)
XLA Modules:
  0.0 134.5 jit_solution(819701158888653095)
XLA Ops:
  0.6 0.0 copy-start
  0.6 0.9 copy.23
  1.6 0.7 pad_clamp_fusion.1
  2.2 0.0 copy-done
  2.2 0.6 gather_fusion
  2.8 0.7 pad_clamp_fusion
  3.5 0.6 gather_fusion.1
  4.1 6.3 %fusion = f32[78,192,128]{2,0,1:T(8,128)S(1)} fusion(s32[192,128]{1,0:T(8,128)S(1)} %bitcast.18, f32[78,30]{1,0:T(8,128)S(1)} %gather_fusion, f32[78,30]{1,0:T(8,128)S(1)} %gather_fusion.1), kind=kOutput, calls=%fused_computation.2 | convolution fusion | flops 692308224 | bytes 7784736 | tf_op jit(solution)/shard_map/qt,tyz->qyz/dot_general | solution.py:263
  10.4 0.0 copy-start.3
  10.4 0.0 copy-start.4
  10.4 5.4 %copy.25.gram = f32[78,192,128]{2,1,0:T(8,128)} copy(f32[78,192,128]{2,0,1:T(8,128)S(1)} %fusion) | data formatting | bytes 15335424 | tf_op jit(solution)/shard_map/qt,tyz->qyz/dot_general | solution.py:263
  15.8 0.0 copy-done.3
  15.8 0.0 copy-done.4
  15.9 36.1 %shard_map.149 = f32[24,4,2,2,8,384]{5,4,3,2,1,0:T(8,128)S(1)} custom-call(f32[2,24,8,384]{3,2,1,0:T(8,128)S(1)} %bitcast.16), custom_call_target="tpu_custom_call" | custom-call | tf_op jit(solution)/shard_map/pallas_call | solution.py:584
  52.1 0.0 copy-start.1
  52.1 2.1 %copy-done.1 = f32[24,4,2,2,8,384]{5,4,3,2,1,0:T(8,128)} copy-done((f32[24,4,2,2,8,384]{5,4,3,2,1,0:T(8,128)}, f32[24,4,2,2,8,384]{5,4,3,2,1,0:T(8,128)S(1)}, u32[]{:S(2)}) %copy-start.1) | copy-done | bytes 4718616
  54.2 50.6 %shard_map.150 = (f32[12,128,384]{2,1,0:T(8,128)}, f32[3,128,384]{2,1,0:T(8,128)}) custom-call(f32[24,128,384]{2,1,0:T(8,128)} %bitcast.14, f32[3,128,384]{2,1,0:T(8,128)} %coil.1, f32[3,128,384]{2,1,0:T(8,128)} %step.2, f32[78,192,128]{2,1,0:T(8,128)} %copy.25.gram, bf16[4,192,576]{2,1,0:T(8,128)(2,1)} %constant.21.clone.yl, ...), custom_call_target="tpu_custom_call" | custom-call | flops 16000000000 | bytes 20971520 | tf_op jit(solution)/shard_map/pallas_call | solution.py:236
  104.8 0.0 copy-start.2
  104.8 1.7 %copy-done.2 = f32[12,128,384]{2,1,0:T(8,128)S(1)} copy-done((f32[12,128,384]{2,1,0:T(8,128)S(1)}, f32[12,128,384]{2,1,0:T(8,128)}, u32[]{:S(2)}) %copy-start.2) | copy-done | bytes 2359320
  106.4 27.4 %shard_map.151 = f32[2,12,8,384]{3,2,1,0:T(8,128)S(1)} custom-call(f32[12,4,2,2,8,384]{5,4,3,2,1,0:T(8,128)S(1)} %bitcast.15, f32[2,12,8,384]{3,2,1,0:T(8,128)S(1)} %copy-done.3), custom_call_target="tpu_custom_call" | custom-call | tf_op jit(solution)/shard_map/pallas_call | solution.py:605
  133.8 0.7 copy.29
  (2 shorter events, 0.1 us)
Async XLA Ops:
  0.6 1.6 %copy-start = (f32[30,12]{0,1:T(8,128)S(1)}, f32[30,12]{0,1:T(8,128)}, u32[]{:S(2)}) copy-start(f32[30,12]{0,1:T(8,128)} %param.18) | copy-start | bytes 4324
  10.4 5.4 %copy-start.3 = (f32[2,12,8,384]{3,2,1,0:T(8,128)S(1)}, f32[2,12,8,384]{3,2,1,0:T(8,128)}, u32[]{:S(2)}) copy-start(f32[2,12,8,384]{3,2,1,0:T(8,128)} %step.3) | copy-start | bytes 884740
  10.4 5.4 %copy-start.4 = (f32[2,12,8,384]{3,2,1,0:T(8,128)S(1)}, f32[2,12,8,384]{3,2,1,0:T(8,128)}, u32[]{:S(2)}) copy-start(f32[2,12,8,384]{3,2,1,0:T(8,128)} %param.14) | copy-start | bytes 884740
  52.1 2.1 %copy-start.1 = (f32[24,4,2,2,8,384]{5,4,3,2,1,0:T(8,128)}, f32[24,4,2,2,8,384]{5,4,3,2,1,0:T(8,128)S(1)}, u32[]{:S(2)}) copy-start(f32[24,4,2,2,8,384]{5,4,3,2,1,0:T(8,128)S(1)} %shard_map.149) | copy-start | bytes 14155780
  104.8 1.7 %copy-start.2 = (f32[12,128,384]{2,1,0:T(8,128)S(1)}, f32[12,128,384]{2,1,0:T(8,128)}, u32[]{:S(2)}) copy-start(f32[12,128,384]{2,1,0:T(8,128)} %get-tuple-element.4) | copy-start | bytes 7077892

commit v2 on v1

--- a/solution.py
+++ b/solution.py
@@ -140,7 +140,7 @@
 def transposed_in(cols, colt, first, count):
     @pl.loop(first, first + count)
     def _(p):
-        colt[p] = cols[p].T.reshape(2, NY, NZ)
+        colt[p] = cols[p].reshape(NZ, 2 * NY).T.reshape(2, NY, NZ)
 
 
 def forward_pass(items, first_pair, pair_count, colt, img, spec, yl, zt):
@@ -170,7 +170,8 @@
             for k in range(COEFS):
                 acc_re = acc_im = None
                 for m in range(COEFS):
-                    g = gram[PAIR_AT[(min(k, m), max(k, m))], rows, :]
+                    first = PAIR_AT[(min(k, m), max(k, m))] * NY + tile * 8
+                    g = gram[pl.ds(pl.multiple_of(first, 8), 8), :]
                     acc_re = g * re[m] if acc_re is None else acc_re + g * re[m]
                     acc_im = g * im[m] if acc_im is None else acc_im + g * im[m]
                 spec[i, k, 0, rows, :] = acc_re
@@ -206,8 +207,8 @@
         back[i, 1] = back_im
 
 
-def coil_gradients(items, back, step_ref, weights, yr, zt, out):
-    @pl.loop(0, items)
+def coil_gradients(first, count, back, step_ref, weights, yr, zt, out):
+    @pl.loop(first, first + count)
     def _(i):
         re, im = z_stage(back[i, 0], back[i, 1], zt[0])
         rows = jnp.concatenate([re, im], axis=0).T
@@ -226,7 +227,7 @@
     def _(k):
         part[k] = grad[k].reshape(2 * NY, NZ).T
 
-    coil_gradients(items, back, step, weights, yr, zt, spec_out)
+    coil_gradients(0, items, back, step, weights, yr, zt, spec_out)
 
 
 def compute(cols, coil, step, gram):
@@ -564,65 +565,139 @@
     return [dma((chunks,))] * 6 + [dma((chunks, 2)), dma((chunks,))]
 
 
-def each(chunks, step):
-    @pl.loop(0, chunks)
-    def _(ch):
-        step(ch)
-
-
-def gather_kernel(chunks, both, cols, *sems):
+PAIR_ROWS = 80
+FRAME_ROWS = 32
+
+
+def gram_operands(temporal_basis, sample_mask):
+    first = np.array([p[0] for p in PAIRS])
+    second = np.array([p[1] for p in PAIRS])
+    pick_first = jnp.asarray(np.eye(COEFS, dtype=np.float32)[first])
+    pick_second = jnp.asarray(np.eye(COEFS, dtype=np.float32)[second])
+    left = jnp.einsum("qk,tk->qt", pick_first, temporal_basis, precision=lax.Precision.HIGHEST)
+    right = jnp.einsum("qk,tk->qt", pick_second, temporal_basis, precision=lax.Precision.HIGHEST)
+    outer = jnp.pad(left * right, ((0, PAIR_ROWS - len(PAIRS)), (0, FRAME_ROWS - FRAMES)))
+    mask = sample_mask.T.reshape(HY, 2, NZ).transpose(1, 0, 2).reshape(NY, NZ)
+    return outer, mask
+
+
+def gram_tiles(first, count, outer, mask, gram):
+    high, low = split(outer[...])
+    least = (outer[...] - high.astype(F32) - low.astype(F32)).astype(BF16)
+    table = jnp.concatenate([high, low, least], axis=1)
+    frame = lax.broadcasted_iota(jnp.int32, (FRAME_ROWS, NZ), 0)
+
+    @pl.loop(first, first + count)
+    def _(tile):
+        words = mask[pl.ds(pl.multiple_of(tile * 8, 8), 8), :]
+        for r in range(0, 8, 2):
+            bits = []
+            for j in range(2):
+                word = jnp.broadcast_to(words[r + j : r + j + 1], (FRAME_ROWS, NZ))
+                bits.append(jnp.bitwise_and(jnp.right_shift(word, frame), 1).astype(F32).astype(BF16))
+            once = jnp.concatenate(bits, axis=1)
+            out = jnp.dot(table, jnp.concatenate([once] * 3, axis=0), preferred_element_type=F32)
+            for j in range(2):
+                gram[pl.ds(tile * 8 + r + j, PAIR_ROWS, stride=NY), :] = out[:, j * NZ : (j + 1) * NZ]
+
+
+def fused_kernel(
+    items, both, coil, step, home, outer, mask, yl, yr, zt, weights, grad_out, spec_out,
+    cols, colt, img, spec, grad, back, part, gram, *rest
+):
+    chunks = COEFS // 2
     at = Place()
     greet(at)
-    g = Gather(at, both, cols, sems, chunks)
-    for step in (g.start, g.on_z, g.on_y, g.on_core, g.finish):
-        each(chunks, step)
-
-
-def gather_near(both):
-    chunks = 3
+    g = Gather(at, both, cols, rest[:8], chunks)
+    s = Scatter(at, part, home, grad_out, rest[8:12], rest[12:], chunks)
+    tiles = NY // 8 // 3
+    for ch in range(3):
+        g.start(ch)
+    gram_tiles(0, tiles, outer, mask, gram)
+    g.on_z(0)
+    g.start(3)
+    gram_tiles(tiles, tiles, outer, mask, gram)
+    g.on_z(1)
+    g.start(4)
+    g.on_y(0)
+    gram_tiles(2 * tiles, tiles, outer, mask, gram)
+    g.on_z(2)
+    g.start(5)
+    g.on_y(1)
+    coil_images(items, coil, step, weights, yr, zt, img)
+    back[...] = jnp.zeros_like(back)
+    for ch in range(chunks):
+        if ch + 3 < chunks:
+            g.on_z(ch + 3)
+        if ch + 2 < chunks:
+            g.on_y(ch + 2)
+        g.on_core(ch)
+        transposed_in(cols, colt, 4 * ch, 4)
+        forward_pass(items, ch, 1, colt, img, spec, yl, zt)
+    for ch in range(chunks):
+        g.finish(ch)
+    mix_pass(items, gram, spec)
+
+    def stages(ch):
+        for late, stage in ((1, s.on_core), (2, s.on_y), (3, s.on_z)):
+            if 0 <= ch - late < chunks:
+                stage(ch - late)
+
+    for ch in range(chunks):
+        inverse_pass(items, ch, 1, colt, img, spec, grad, back, yl, zt)
+        for k in (2 * ch, 2 * ch + 1):
+            part[k] = grad[k].reshape(2 * NY, NZ).T.reshape(4, 2, 2, 8, 2 * NY)
+        s.start(ch)
+        stages(ch)
+    for i in range(items):
+        coil_gradients(i, 1, back, step, weights, yr, zt, spec_out)
+        stages(chunks + i)
+    for ch in range(chunks + items, chunks + 3):
+        stages(ch)
+    for ch in range(chunks):
+        s.on_far(ch)
+    for ch in range(chunks):
+        s.finish(ch)
+
+
+def fused(both, coil, step, home, outer, mask):
+    items = coil.shape[0]
+    chunks = COEFS // 2
+    tables = make_tables()
     vmem = pl.BlockSpec(memory_space=pltpu.VMEM)
     return pl.pallas_call(
-        functools.partial(gather_kernel, chunks),
-        out_shape=jax.ShapeDtypeStruct((2 * COEFS, 4, 2, 2, 8, 2 * NY), F32),
-        in_specs=[vmem],
-        out_specs=vmem,
-        scratch_shapes=gather_sems(chunks),
-        compiler_params=pltpu.CompilerParams(collective_id=0, has_side_effects=True, vmem_limit_bytes=32 * 2**20),
-    )(both)
-
-
-def scatter_kernel(chunks, part, step, out, *scratch):
-    at = Place()
-    greet(at)
-    s = Scatter(at, part, step, out, scratch[:4], scratch[4:], chunks)
-    for stage in (s.start, s.on_core, s.on_y, s.on_z, s.on_far, s.finish):
-        each(chunks, stage)
-
-
-def scatter_near(part, step):
-    chunks = 3
-    vmem = pl.BlockSpec(memory_space=pltpu.VMEM)
-    return pl.pallas_call(
-        functools.partial(scatter_kernel, chunks),
-        out_shape=jax.ShapeDtypeStruct(step.shape, F32),
-        in_specs=[vmem] * 2,
-        out_specs=vmem,
-        scratch_shapes=scatter_scratch() + scatter_sems(chunks),
-        compiler_params=pltpu.CompilerParams(collective_id=1, has_side_effects=True, vmem_limit_bytes=32 * 2**20),
-    )(part, step)
+        functools.partial(fused_kernel, items),
+        out_shape=(jax.ShapeDtypeStruct(home.shape, F32), jax.ShapeDtypeStruct(coil.shape, F32)),
+        in_specs=[vmem] * 10,
+        out_specs=(vmem, vmem),
+        scratch_shapes=[
+            pltpu.VMEM((2 * COEFS, 4, 2, 2, 8, 2 * NY), F32),
+            pltpu.VMEM((2 * COEFS, 2, NY, NZ), F32),
+            pltpu.VMEM((items, 2, 2, NY, NZ), F32),
+            pltpu.VMEM((items, COEFS, 2, NY, NZ), F32),
+            pltpu.VMEM((COEFS, 2, NY, NZ), F32),
+            pltpu.VMEM((items, 2, NY, NZ), F32),
+            pltpu.VMEM((COEFS, 4, 2, 2, 8, 2 * NY), F32),
+            pltpu.VMEM((PAIR_ROWS * NY, NZ), F32),
+        ]
+        + gather_sems(chunks)
+        + scatter_scratch()
+        + scatter_sems(chunks),
+        compiler_params=pltpu.CompilerParams(collective_id=0, has_side_effects=True, vmem_limit_bytes=56 * 2**20),
+        cost_estimate=pl.CostEstimate(flops=16 * 10**9, bytes_accessed=20 * 2**20, transcendentals=0),
+    )(both, coil, step, home, outer, mask, *[jnp.asarray(t) for t in tables])
 
 
 def shards(image_coef, step_coef, coil_spec, step_spec, temporal_basis, sample_mask):
     devices = lax.axis_size("slab")
     width_x, _, rows_z, _ = image_coef.shape
     both = jnp.stack([image_coef, step_coef], axis=2).reshape(width_x, 2 * COEFS, rows_z, 2 * NY)
-    gram = gram_planes(temporal_basis, sample_mask)
     if devices == 16 and width_x == 2 and rows_z == 8:
-        cols = gather_near(both).reshape(2 * COEFS, NZ, 2 * NY)
-        part, grad_spec = compute(cols, coil_spec, step_spec, gram)
-        grad_coef = scatter_near(part.reshape(COEFS, 4, 2, 2, rows_z, 2 * NY), step_coef)
+        outer, mask = gram_operands(temporal_basis, sample_mask)
+        return fused(both, coil_spec, step_spec, step_coef, outer, mask)
     else:
         cols = gather_plain(both, devices)
+        gram = gram_planes(temporal_basis, sample_mask).reshape(len(PAIRS) * NY, NZ)
         part, grad_spec = compute(cols, coil_spec, step_spec, gram)
         grad_coef = scatter_plain(part, width_x, devices) + ALPHA * step_coef
     return grad_coef, grad_spec

time: 135 us -> 98.9 us (0.73)
  Pallas kernels: 114 us -> 87.3 us
  local copies, waits for them, and re-layouts: 12.1 us -> 7.44 us
  matrix products: 6.32 us -> 1.99 us
    pallas_call x3 -> x1, Pallas kernels: 114 us -> 87.3 us  [fused(): pl.pallas_call(functools.partial(fused_kernel, items), out_shape=(jax.Sha...]
    dot_general x1 -> x0, local copies, waits for them, and re-layouts: 5.37 us -> none  [gram_planes(): jnp.einsum('qt,tyz->qyz', outer, bits, precision=lax.Precision.HIGHEST)]
    dot_general x1 -> x2, matrix products: 6.32 us -> 1.99 us  [the longest x1 1.01 us: gram_operands(): jnp.einsum('qk,tk->qt', pick_second, temporal_basis, precision=lax.Precis...]
    reshape x0 -> x1, local copies, waits for them, and re-layouts: none -> 1.54 us  [gram_operands(): mask = sample_mask.T.reshape(HY, 2, NZ).transpose(1, 0, 2).reshape(NY, NZ)]
    unnamed x11 -> x4, local copies, waits for them, and re-layouts: 4.54 us -> 4.31 us
where the time goes in v2:
time: 98.9 us; the launch traced here: 98.5 us
  Pallas kernels  87.3 us (88%)
  local copies, waits for them, and re-layouts  7.44 us (8%)
  matrix products  1.99 us (2%)
  other arithmetic  1.09 us (1%)
    pallas_call x1, Pallas kernels, fused(): pl.pallas_call(functools.partial(fused_kernel, items), out_shape=(jax.Sha...  87.3 us
    unnamed x4, local copies, waits for them, and re-layouts  4.31 us

profile of v2, /device:TPU:0, one launch (start us, length us, event | category | flops | bytes accessed | tf_op | source)
XLA Modules:
  0.0 98.5 jit_solution(304184444031910598)
XLA Ops:
  0.6 0.0 copy-start
  0.6 0.7 copy-done
  1.3 1.0 %fusion = f32[78,30]{0,1:T(8,128)S(1)} fusion(f32[78,12]{1,0:T(8,128)} %constant.15.clone, f32[30,12]{0,1:T(8,128)S(1)} %copy-done), kind=kOutput, calls=%fused_computation.2 | convolution fusion | flops 336960 | bytes 14544 | tf_op jit(solution)/shard_map/qk,tk->qt/dot_general | solution.py:577
  2.3 1.0 %convolution_multiply_fusion = f32[78,30]{0,1:T(8,128)S(1)} fusion(f32[78,30]{0,1:T(8,128)S(1)} %fusion, f32[78,12]{1,0:T(8,128)} %constant.16.clone, f32[30,12]{0,1:T(8,128)S(1)} %copy-done), kind=kOutput, calls=%fused_computation | convolution fusion | flops 339300 | bytes 23904 | tf_op jit(solution)/shard_map/qk,tk->qt/dot_general | solution.py:578
  3.4 0.1 copy.19
  3.5 0.6 pad.4.outer
  4.1 1.5 %copy.20 = s32[96,2,128]{2,0,1:T(8,128)} copy(s32[96,2,128]{2,1,0:T(2,128)} %bitcast.16) | data formatting | bytes 196608 | tf_op jit(solution)/shard_map/reshape | solution.py:580
  5.6 1.1 %pad_maximum_fusion = f32[2,12,2,8,384]{4,3,1,0,2:T(8,128)S(1)} fusion(f32[2,12,1,8,384]{4,3,1,0,2:T(8,128)} %bitcast.15, f32[2,12,1,8,384]{4,3,1,0,2:T(8,128)} %bitcast.14), kind=kLoop, calls=%fused_computation.1 | loop fusion | flops 147456 | bytes 1179648 | tf_op jit(solution)/shard_map/stack | solution.py:694
  6.7 0.9 copy.18
  7.6 87.3 %shard_map.131 = (f32[2,12,8,384]{3,2,1,0:T(8,128)}, f32[3,128,384]{2,1,0:T(8,128)}) custom-call(f32[2,24,8,384]{3,2,1,0:T(8,128)} %bitcast.13, f32[3,128,384]{2,1,0:T(8,128)} %coil.1, f32[3,128,384]{2,1,0:T(8,128)} %step.1, f32[2,12,8,384]{3,2,1,0:T(8,128)} %home.1, f32[80,32]{1,0:T(8,128)} %pad.4.outer, s32[192,128]{1,0:T(8,128)} %bitcast.17, ...), custom_call_target="tpu_custom_call" | custom-call | flops 16000000000 | bytes 20971520 | tf_op jit(solution)/shard_map/pallas_call | solution.py:668
  94.9 1.7 %copy.23 = f32[2,12,8,384]{3,2,1,0:T(8,128)} copy(f32[2,12,8,384]{3,2,1,0:T(8,128)} %get-tuple-element.4) | data formatting | bytes 589824
  96.6 1.9 %copy.24 = f32[3,128,384]{2,1,0:T(8,128)} copy(f32[3,128,384]{2,1,0:T(8,128)} %get-tuple-element.5) | data formatting | bytes 1179648
Async XLA Ops:
  0.6 0.7 copy-start

commit v3 on v2

--- a/solution.py
+++ b/solution.py
@@ -138,13 +138,13 @@
 
 
 def transposed_in(cols, colt, first, count):
-    @pl.loop(first, first + count)
+    @pl.loop(first, first + count, unroll=2)
     def _(p):
         colt[p] = cols[p].reshape(NZ, 2 * NY).T.reshape(2, NY, NZ)
 
 
 def forward_pass(items, first_pair, pair_count, colt, img, spec, yl, zt):
-    @pl.loop(first_pair * items, (first_pair + pair_count) * items)
+    @pl.loop(first_pair * items, (first_pair + pair_count) * items, unroll=items if pair_count == 1 else None)
     def _(step):
         pair, i = step // items, step % items
         planes = []
@@ -179,7 +179,7 @@
 
 
 def inverse_pass(items, first_pair, pair_count, colt, img, spec, grad, back, yl, zt):
-    @pl.loop(first_pair * items, (first_pair + pair_count) * items)
+    @pl.loop(first_pair * items, (first_pair + pair_count) * items, unroll=items if pair_count == 1 else None)
     def _(step):
         pair, i = step // items, step % items
         outs = inverse([(spec[i, 2 * pair + j, 0], spec[i, 2 * pair + j, 1]) for j in range(2)], yl, zt)
@@ -572,18 +572,17 @@
 def gram_operands(temporal_basis, sample_mask):
     first = np.array([p[0] for p in PAIRS])
     second = np.array([p[1] for p in PAIRS])
-    pick_first = jnp.asarray(np.eye(COEFS, dtype=np.float32)[first])
-    pick_second = jnp.asarray(np.eye(COEFS, dtype=np.float32)[second])
-    left = jnp.einsum("qk,tk->qt", pick_first, temporal_basis, precision=lax.Precision.HIGHEST)
-    right = jnp.einsum("qk,tk->qt", pick_second, temporal_basis, precision=lax.Precision.HIGHEST)
-    outer = jnp.pad(left * right, ((0, PAIR_ROWS - len(PAIRS)), (0, FRAME_ROWS - FRAMES)))
+    picks = np.zeros((2 * PAIR_ROWS, COEFS), np.float32)
+    picks[np.arange(len(PAIRS)), first] = 1.0
+    picks[PAIR_ROWS + np.arange(len(PAIRS)), second] = 1.0
+    basis = jnp.pad(temporal_basis, ((0, FRAME_ROWS - FRAMES), (0, 0)))
     mask = sample_mask.T.reshape(HY, 2, NZ).transpose(1, 0, 2).reshape(NY, NZ)
-    return outer, mask
+    return basis, jnp.asarray(picks), mask
 
 
 def gram_tiles(first, count, outer, mask, gram):
-    high, low = split(outer[...])
-    least = (outer[...] - high.astype(F32) - low.astype(F32)).astype(BF16)
+    high, low = split(outer)
+    least = (outer - high.astype(F32) - low.astype(F32)).astype(BF16)
     table = jnp.concatenate([high, low, least], axis=1)
     frame = lax.broadcasted_iota(jnp.int32, (FRAME_ROWS, NZ), 0)
 
@@ -602,7 +601,7 @@
 
 
 def fused_kernel(
-    items, both, coil, step, home, outer, mask, yl, yr, zt, weights, grad_out, spec_out,
+    items, both, coil, step, home, basis, picks, mask, yl, yr, zt, weights, grad_out, spec_out,
     cols, colt, img, spec, grad, back, part, gram, *rest
 ):
     chunks = COEFS // 2
@@ -613,6 +612,10 @@
     tiles = NY // 8 // 3
     for ch in range(3):
         g.start(ch)
+    picked = lax.dot_general(
+        picks[...], basis[...], (((1,), (1,)), ((), ())), precision=lax.Precision.HIGHEST, preferred_element_type=F32
+    )
+    outer = picked[:PAIR_ROWS] * picked[PAIR_ROWS:]
     gram_tiles(0, tiles, outer, mask, gram)
     g.on_z(0)
     g.start(3)
@@ -660,7 +663,7 @@
         s.finish(ch)
 
 
-def fused(both, coil, step, home, outer, mask):
+def fused(both, coil, step, home, basis, picks, mask):
     items = coil.shape[0]
     chunks = COEFS // 2
     tables = make_tables()
@@ -668,7 +671,7 @@
     return pl.pallas_call(
         functools.partial(fused_kernel, items),
         out_shape=(jax.ShapeDtypeStruct(home.shape, F32), jax.ShapeDtypeStruct(coil.shape, F32)),
-        in_specs=[vmem] * 10,
+        in_specs=[vmem] * 11,
         out_specs=(vmem, vmem),
         scratch_shapes=[
             pltpu.VMEM((2 * COEFS, 4, 2, 2, 8, 2 * NY), F32),
@@ -685,7 +688,7 @@
         + scatter_sems(chunks),
         compiler_params=pltpu.CompilerParams(collective_id=0, has_side_effects=True, vmem_limit_bytes=56 * 2**20),
         cost_estimate=pl.CostEstimate(flops=16 * 10**9, bytes_accessed=20 * 2**20, transcendentals=0),
-    )(both, coil, step, home, outer, mask, *[jnp.asarray(t) for t in tables])
+    )(both, coil, step, home, basis, picks, mask, *[jnp.asarray(t) for t in tables])
 
 
 def shards(image_coef, step_coef, coil_spec, step_spec, temporal_basis, sample_mask):
@@ -693,8 +696,8 @@
     width_x, _, rows_z, _ = image_coef.shape
     both = jnp.stack([image_coef, step_coef], axis=2).reshape(width_x, 2 * COEFS, rows_z, 2 * NY)
     if devices == 16 and width_x == 2 and rows_z == 8:
-        outer, mask = gram_operands(temporal_basis, sample_mask)
-        return fused(both, coil_spec, step_spec, step_coef, outer, mask)
+        basis, picks, mask = gram_operands(temporal_basis, sample_mask)
+        return fused(both, coil_spec, step_spec, step_coef, basis, picks, mask)
     else:
         cols = gather_plain(both, devices)
         gram = gram_planes(temporal_basis, sample_mask).reshape(len(PAIRS) * NY, NZ)

time: 98.9 us -> 93.1 us (0.941)
  Pallas kernels: 87.3 us -> 83.7 us
  matrix products: 1.99 us -> 0 us
    pallas_call x1, Pallas kernels: 87.3 us -> 83.7 us  [fused(): pl.pallas_call(functools.partial(fused_kernel, items), out_shape=(jax.Sha...]
    dot_general x2 -> x0, matrix products: 1.99 us -> none  [the longest x1 1.01 us: gram_operands(): jnp.einsum('qk,tk->qt', pick_second, temporal_basis, precision=lax.Precis...]
    unnamed x4 -> x3, local copies, waits for them, and re-layouts: 4.31 us -> 4.4 us
where the time goes in v3:
time: 93.1 us; the launch traced here: 92.8 us
  Pallas kernels  83.7 us (90%)
  local copies, waits for them, and re-layouts  7.4 us (8%)
  other arithmetic  1.09 us (1%)
    pallas_call x1, Pallas kernels, fused(): pl.pallas_call(functools.partial(fused_kernel, items), out_shape=(jax.Sha...  83.7 us
    unnamed x3, local copies, waits for them, and re-layouts  4.4 us

profile of v3, /device:TPU:0, one launch (start us, length us, event | category | flops | bytes accessed | tf_op | source)
XLA Modules:
  0.0 92.8 jit_solution(8849874388809786109)
XLA Ops:
  0.6 0.8 copy.14
  1.4 0.6 pad.4.basis
  2.0 1.5 %copy.15 = s32[96,2,128]{2,0,1:T(8,128)} copy(s32[96,2,128]{2,1,0:T(2,128)} %bitcast.12) | data formatting | bytes 196608 | tf_op jit(solution)/shard_map/reshape | solution.py:579
  3.6 1.1 %pad_maximum_fusion = f32[2,12,2,8,384]{4,3,1,0,2:T(8,128)S(1)} fusion(f32[2,12,1,8,384]{4,3,1,0,2:T(8,128)} %bitcast.11, f32[2,12,1,8,384]{4,3,1,0,2:T(8,128)} %bitcast.10), kind=kLoop, calls=%fused_computation | loop fusion | flops 147456 | bytes 1179648 | tf_op jit(solution)/shard_map/stack | solution.py:697
  4.7 0.9 copy.13
  5.5 83.7 %shard_map.122 = (f32[2,12,8,384]{3,2,1,0:T(8,128)}, f32[3,128,384]{2,1,0:T(8,128)}) custom-call(f32[2,24,8,384]{3,2,1,0:T(8,128)} %bitcast.9, f32[3,128,384]{2,1,0:T(8,128)} %coil.1, f32[3,128,384]{2,1,0:T(8,128)} %step.1, f32[2,12,8,384]{3,2,1,0:T(8,128)} %home.1, f32[32,12]{1,0:T(8,128)} %pad.4.basis, f32[160,12]{1,0:T(8,128)} %constant.13.clone.picks, ...), custom_call_target="tpu_custom_call" | custom-call | flops 16000000000 | bytes 20971520 | tf_op jit(solution)/shard_map/pallas_call | solution.py:671
  89.2 1.7 %copy.18 = f32[2,12,8,384]{3,2,1,0:T(8,128)} copy(f32[2,12,8,384]{3,2,1,0:T(8,128)} %get-tuple-element.4) | data formatting | bytes 589824
  90.9 1.9 %copy.19 = f32[3,128,384]{2,1,0:T(8,128)} copy(f32[3,128,384]{2,1,0:T(8,128)} %get-tuple-element.5) | data formatting | bytes 1179648
